TPU v7x, 32 devices: a whole 2x2x4 slice. The times are simulated.
32 devices in a mesh: bx: 4 (over z), by: 8 (over y, x, core).
Axes of the slice: x: 2, y: 2, z: 4, core: 2. Of those that a mesh axis runs over, the one named last changes fastest.
Arguments:
- positions: float32 [3, 4096], P(None, ('bx', 'by')), may hold values from 0 to 8, as said below
- tangent: float32 [3, 4096], P(None, ('bx', 'by')), may hold values from -6 to 6
- embedding: float32 [4096, 256], P(('bx', 'by')), may hold values from -6 to 6
- counts: int32 [32], P(('bx', 'by')), may hold values from 64 to 128, as said below
- neighbours: int32 [32, 4096], P(None, ('bx', 'by')), may hold values from 0 to 191, as said below
- send_rows: int32 [32, 64], P(('bx', 'by')), may hold values from 0 to 127
- w_one_in: float32 [256, 256], replicated, may hold values from -0.375 to 0.375
- w_one_out: float32 [256, 512], replicated, may hold values from -0.375 to 0.375
- filter_one: float32 [20, 512], replicated, may hold values from -0.3125 to 0.3125
- w_left: float32 [256, 256], replicated, may hold values from -0.375 to 0.375
- w_right: float32 [256, 256], replicated, may hold values from -0.375 to 0.375
- w_two_in: float32 [256, 256], replicated, may hold values from -0.375 to 0.375
- w_two_out: float32 [256, 256], replicated, may hold values from -0.375 to 0.375
- filter_two: float32 [20, 256], replicated, may hold values from -0.3125 to 0.3125
- w_hidden: float32 [256, 256], replicated, may hold values from -0.375 to 0.375
- w_energy: float32 [256], replicated, may hold values from -0.375 to 0.375
Outputs:
- forces: float32 [3, 4096], P(None, ('bx', 'by'))
- hessian_tangent: float32 [3, 4096], P(None, ('bx', 'by'))
Inputs may be any that keep to these rules, and one draw needn't show every extreme that they name: The live atoms of a brick are its first counts rows; every count is a multiple of 32; some brick holds 128 live atoms and some 128 // 2. `neighbours`: the 32 slots of an atom are distinct; each is a live row of its own brick other than the atom's own row, or a slot of a neighbouring brick that exists in the sheet. `positions`: atom n lies within one unit of its brick's indices along x and y, with the third coordinate in [0, 0.3).
All inputs are finite; a program needn't handle non-finite values.
Results may differ from a plain program's by a relative error of at most 0.0003.
Values sent between devices are 32-bit elements; how exact they have to be, the bound alone decides.
No kernel may reach another device: no remote copies, remote signals or barrier semaphores. Data moves between devices by JAX's collectives and lax.ppermute only.
A program may use at most 192 MiB of HBM per device.

v0:
```python
import math

import jax
import jax.numpy as jnp
from jax import lax
from jax.sharding import PartitionSpec as P

highest = lax.Precision.HIGHEST
cutoff_radius = 3.0
softening = 0.01
offsets = ((-1, -1), (-1, 0), (-1, 1), (0, -1), (0, 1), (1, -1), (1, 0), (1, 1))


def passed_along(block, axis, distance):
    devices = range(lax.axis_size(axis))
    route = [(i - distance, i) for i in devices if i - distance in devices]
    return lax.ppermute(block, axis, route)


def project_rows(features, w_inner, w_outer):
    inner = jax.nn.silu(jnp.dot(features, w_inner, precision=highest))
    return jnp.dot(inner, w_outer, precision=highest)


def geometry(pos_table, own_lists, basis_count):
    own_rows = own_lists.shape[1]
    centre = pos_table[:, :own_rows]
    others = jnp.take(pos_table, own_lists, axis=1)
    offset = others - centre[:, None, :]
    distance = jnp.sqrt(jnp.sum(offset * offset, axis=0) + softening)
    direction = offset / distance[None]
    orders = jnp.arange(1, basis_count + 1).astype(distance.dtype)
    radial = (
        jnp.sin(orders[:, None, None] * (math.pi / cutoff_radius) * distance[None]) / distance[None]
    )
    envelope = 0.5 * (jnp.cos(math.pi / cutoff_radius * distance) + 1.0)
    return (radial, envelope, direction)


def edge_weights(radial, envelope, filter_table):
    mixed = jnp.einsum("qkr,qc->krc", radial, filter_table, precision=highest)
    return mixed * envelope[:, :, None]


def first_layer(pos_table, phi_table, embed_own, own_lists, filter_one, w_left, w_right):
    radial, envelope, direction = geometry(pos_table, own_lists, filter_one.shape[0])
    scale_edges = 1.0 / math.sqrt(own_lists.shape[0])
    message = jnp.take(phi_table, own_lists, axis=0) * edge_weights(radial, envelope, filter_one)
    channels = embed_own.shape[1]
    scalar_part = scale_edges * jnp.sum(message[:, :, :channels], axis=0)
    vector_part = scale_edges * jnp.einsum(
        "ckr,krf->crf", direction, message[:, :, channels:], precision=highest
    )
    left_map = jnp.einsum("crf,fg->crg", vector_part, w_left, precision=highest)
    right_map = jnp.einsum("crf,fg->crg", vector_part, w_right, precision=highest)
    return embed_own + scalar_part + jnp.sum(left_map * right_map, axis=0)


def second_layer(
    pos_table, phi_table, state_own, own_lists, live_rows, filter_two, w_hidden, w_energy
):
    geometry_parts = geometry(pos_table, own_lists, filter_two.shape[0])
    scale_edges = 1.0 / math.sqrt(own_lists.shape[0])
    weighted = jnp.take(phi_table, own_lists, axis=0) * edge_weights(
        geometry_parts[0], geometry_parts[1], filter_two
    )
    message = scale_edges * jnp.sum(weighted, axis=0)
    hidden_rows = jax.nn.silu(jnp.dot(state_own + message, w_hidden, precision=highest))
    return jnp.sum(live_rows * jnp.dot(hidden_rows, w_energy, precision=highest))


def move_bx(payload, stride):
    return passed_along(payload, "bx", stride)


def move_by(payload, stride):
    return passed_along(payload, "by", stride)


def back_bx(payload, stride):
    return passed_along(payload, "bx", stride)


def back_by(payload, stride):
    return passed_along(payload, "by", stride)


def place_at(along_first, along_second):
    return (along_first, along_second)


def joined(portions, members):
    return tuple(
        (jnp.concatenate([portion[column] for portion in portions], 0) for column in range(members))
    )


def take_block(arrived, number, ghost_count):
    return tuple((member[number * ghost_count : (number + 1) * ghost_count] for member in arrived))


def spread(payload, send_index, moves):
    ghost_count = send_index.shape[0] // 8
    members = len(payload)

    def toward(target):
        number = offsets.index(target)
        chosen = send_index[number * ghost_count : (number + 1) * ghost_count]
        return tuple((jnp.take(member, chosen, axis=0) for member in payload))

    by_slot = {}
    carried = {}
    for heading in (1, -1):
        portions = [toward(place_at(heading, across)) for across in (-1, 0, 1)]
        arrived = moves[0](joined(portions, members), heading)
        by_slot[place_at(-heading, 0)] = take_block(arrived, 1, ghost_count)
        carried[heading, -1] = take_block(arrived, 0, ghost_count)
        carried[heading, 1] = take_block(arrived, 2, ghost_count)
    for across in (1, -1):
        portions = [toward(place_at(0, across)), carried[1, across], carried[-1, across]]
        arrived = moves[1](joined(portions, members), across)
        by_slot[place_at(0, -across)] = take_block(arrived, 0, ghost_count)
        by_slot[place_at(-1, -across)] = take_block(arrived, 1, ghost_count)
        by_slot[place_at(1, -across)] = take_block(arrived, 2, ghost_count)
    return tuple(
        (
            jnp.concatenate([by_slot[target][column] for target in offsets], 0)
            for column in range(members)
        )
    )


def gather_back(payload, send_index, own_rows, moves):
    ghost_count = send_index.shape[0] // 8
    members = len(payload)

    def from_slot(target):
        number = offsets.index(target)
        return tuple(
            (member[number * ghost_count : (number + 1) * ghost_count] for member in payload)
        )

    toward_cot = {}
    carried = {}
    for across in (1, -1):
        portions = [
            from_slot(place_at(0, -across)),
            from_slot(place_at(-1, -across)),
            from_slot(place_at(1, -across)),
        ]
        arrived = moves[1](joined(portions, members), -across)
        toward_cot[place_at(0, across)] = take_block(arrived, 0, ghost_count)
        carried[1, across] = take_block(arrived, 1, ghost_count)
        carried[-1, across] = take_block(arrived, 2, ghost_count)
    for heading in (1, -1):
        portions = [carried[heading, -1], from_slot(place_at(-heading, 0)), carried[heading, 1]]
        arrived = moves[0](joined(portions, members), -heading)
        toward_cot[place_at(heading, -1)] = take_block(arrived, 0, ghost_count)
        toward_cot[place_at(heading, 0)] = take_block(arrived, 1, ghost_count)
        toward_cot[place_at(heading, 1)] = take_block(arrived, 2, ghost_count)
    summed = []
    for column in range(members):
        values = jnp.concatenate([toward_cot[target][column] for target in offsets], 0)
        summed.append(
            jnp.zeros((own_rows, values.shape[1]), values.dtype).at[send_index].add(values)
        )
    return tuple(summed)


def per_device(
    positions,
    tangent,
    embedding,
    counts,
    neighbours,
    send_rows,
    w_one_in,
    w_one_out,
    filter_one,
    w_left,
    w_right,
    w_two_in,
    w_two_out,
    filter_two,
    w_hidden,
    w_energy,
):
    own_rows = positions.shape[1]
    send_index = send_rows[0]
    live_rows = (jnp.arange(own_rows) < counts[0]).astype(jnp.float32)
    forward_moves = (move_bx, move_by)
    return_moves = (back_bx, back_by)
    coords_pack = jnp.concatenate([positions.T, tangent.T], 1)
    phi_own = project_rows(embedding, w_one_in, w_one_out)
    ghost_coords, ghost_phi = spread((coords_pack, phi_own), send_index, forward_moves)
    phi_table = jnp.concatenate([phi_own, ghost_phi], 0)
    pos_table = jnp.concatenate([positions, ghost_coords[:, :3].T], 1)
    tan_table = jnp.concatenate([tangent, ghost_coords[:, 3:].T], 1)

    def first_section(pos_arg):
        return first_layer(pos_arg, phi_table, embedding, neighbours, filter_one, w_left, w_right)

    node_state, state_tangent = jax.jvp(first_section, (pos_table,), (tan_table,))

    def second_rows(state_arg):
        return project_rows(state_arg, w_two_in, w_two_out)

    phi_two, phi_two_tangent = jax.jvp(second_rows, (node_state,), (state_tangent,))
    ghost_two, ghost_two_tangent = spread((phi_two, phi_two_tangent), send_index, forward_moves)
    phi_two_table = jnp.concatenate([phi_two, ghost_two], 0)
    phi_two_tangents = jnp.concatenate([phi_two_tangent, ghost_two_tangent], 0)

    def second_section(pos_arg, phi_arg, state_arg):
        return second_layer(
            pos_arg, phi_arg, state_arg, neighbours, live_rows, filter_two, w_hidden, w_energy
        )

    grads_two, tangents_two = jax.jvp(
        jax.grad(second_section, argnums=(0, 1, 2)),
        (pos_table, phi_two_table, node_state),
        (tan_table, phi_two_tangents, state_tangent),
    )
    pos_grad, pos_grad_tangent = (grads_two[0], tangents_two[0])
    ghost_pack = jnp.concatenate([pos_grad[:, own_rows:].T, pos_grad_tangent[:, own_rows:].T], 1)
    returned = gather_back(
        (grads_two[1][own_rows:], tangents_two[1][own_rows:], ghost_pack),
        send_index,
        own_rows,
        return_moves,
    )
    phi_cot = grads_two[1][:own_rows] + returned[0]
    phi_cot_tangent = tangents_two[1][:own_rows] + returned[1]

    def pull_second(state_arg, cot_arg):
        pullback = jax.vjp(second_rows, state_arg)[1]
        return pullback(cot_arg)[0]

    extra_cot, extra_tangent = jax.jvp(
        pull_second, (node_state, phi_cot), (state_tangent, phi_cot_tangent)
    )
    state_cot = grads_two[2] + extra_cot
    state_cot_tangent = tangents_two[2] + extra_tangent

    def pull_first(pos_arg, cot_arg):
        pullback = jax.vjp(first_section, pos_arg)[1]
        return pullback(cot_arg)[0]

    first_grad, first_grad_tangent = jax.jvp(
        pull_first, (pos_table, state_cot), (tan_table, state_cot_tangent)
    )
    first_pack = jnp.concatenate(
        [first_grad[:, own_rows:].T, first_grad_tangent[:, own_rows:].T], 1
    )
    returned_last = gather_back((first_pack,), send_index, own_rows, return_moves)
    summed = (
        pos_grad[:, :own_rows]
        + first_grad[:, :own_rows]
        + returned[2][:, :3].T
        + returned_last[0][:, :3].T
    )
    summed_tangent = (
        pos_grad_tangent[:, :own_rows]
        + first_grad_tangent[:, :own_rows]
        + returned[2][:, 3:].T
        + returned_last[0][:, 3:].T
    )
    return (-summed, -summed_tangent)


def solution(mesh):
    placed = (
        P(None, ("bx", "by")),
        P(None, ("bx", "by")),
        P(("bx", "by"), None),
        P(("bx", "by")),
        P(None, ("bx", "by")),
        P(("bx", "by"), None),
        P(),
        P(),
        P(),
        P(),
        P(),
        P(),
        P(),
        P(),
        P(),
        P(),
    )
    return jax.shard_map(
        per_device,
        mesh=mesh,
        in_specs=placed,
        out_specs=(P(None, ("bx", "by")), P(None, ("bx", "by"))),
        check_vma=False,
    )
```

profile of v0, /device:TPU:4, one launch (start us, length us, event | category | flops | bytes accessed | tf_op | source)
XLA Modules:
  0.0 594.5 jit_solution(1266530487996895763)
XLA Ops:
  41.1 10.8 %gather_fusion.10 = f32[4096,3]{1,0:T(8,128)S(1)} fusion(f32[3,192]{0,1:T(8,128)S(1)} %copy.337, s32[4096]{0:T(1024)S(1)} %broadcast_clamp_fusion), kind=kCustom, calls=%fused_computation.1.clone | custom fusion | bytes 114688 | tf_op jit(solution)/shard_map/jvp(jvp(jit(_take)))/gather | solution.py:28
  53.3 14.2 %gather_fusion.11 = f32[4096,3]{1,0:T(8,128)} fusion(f32[3,192]{0,1:T(8,128)S(1)} %copy.367, s32[4096]{0:T(1024)S(1)} %broadcast_clamp_fusion), kind=kCustom, calls=%fused_computation.2.clone | custom fusion | bytes 114688 | tf_op jit(solution)/shard_map/jvp(jvp(jit(_take)))/gather | solution.py:28
  71.1 10.4 %fusion.156 = f32[32,128,512]{2,1,0:T(8,128)} fusion(f32[32,128]{1,0:T(8,128)S(1)} %get-tuple-element.134, f32[32,128]{1,0:T(8,128)S(1)} %get-tuple-element.111, f32[32,128]{1,0:T(8,128)S(1)} %get-tuple-element.112, f32[32,128]{1,0:T(8,128)S(1)} %get-tuple-element.135, f32[20]{0:T(128)S(1)} %convert_multiply_fusion, f32[20,512]{1,0:T(8,128)S(1)} %copy-done.48), kind=kOutput, calls=%fused_computation.233 | convolution fusion | flops 503889920 | bytes 8495184 | tf_op jit(solution)/shard_map/jvp(qkr,qc->krc)/dot_general | solution.py:41
  81.5 14.3 %collective-permute-start.6 = (f32[24,512]{1,0:T(8,128)S(1)}, f32[24,512]{1,0:T(8,128)S(1)}, u32[]{:S(2)}, u32[]{:S(2)}) collective-permute-start(f32[24,512]{1,0:T(8,128)S(1)} %pad_maximum_fusion.2), channel_id=1, source_target_pairs={{0,1},{1,2},{2,3},{3,4},{4,5},{5,6},{6,7},{8,9},{9,10},{10,11},{11... | collective-permute-start | bytes 147464 | tf_op jit(solution)/shard_map/ppermute | solution.py:17
  95.9 6.5 %fusion.158 = f32[32,128,256]{2,1,0:T(8,128)} fusion(f32[32,128]{1,0:T(8,128)S(1)} %get-tuple-element.134, f32[32,128]{1,0:T(8,128)S(1)} %get-tuple-element.111, f32[32,128]{1,0:T(8,128)S(1)} %get-tuple-element.112, f32[32,128]{1,0:T(8,128)S(1)} %get-tuple-element.135, f32[20]{0:T(128)S(1)} %convert_multiply_fusion, f32[20,256]{1,0:T(8,128)S(1)} %copy-done.66), kind=kOutput, calls=%fused_computation.234 | convolution fusion | flops 252231680 | bytes 4280400 | tf_op jit(solution)/shard_map/jvp(jvp(qkr,qc->krc))/dot_general | solution.py:41
  109.0 16.8 %gather_fusion.20 = f32[4096,512]{1,0:T(8,128)} fusion(f32[192,512]{1,0:T(8,128)S(1)} %constant_dynamic-update-slice_fusion, s32[4096]{0:T(1024)S(1)} %broadcast_clamp_fusion), kind=kCustom, calls=%fused_computation.4.clone | custom fusion | bytes 16793600 | tf_op jit(solution)/shard_map/jvp(jit(_take))/gather | solution.py:48
  125.9 15.0 %add_multiply_fusion.1 = (f32[32,128,512]{2,1,0:T(8,128)S(1)}, f32[32,128,512]{2,1,0:T(8,128)S(1)}, f32[32,128,512]{2,1,0:T(8,128)}) fusion(f32[32,128,512]{2,1,0:T(8,128)} %fusion.156, f32[32,128]{1,0:T(8,128)S(1)} %get-tuple-element.110, f32[32,128]{1,0:T(8,128)S(1)} %get-tuple-element.133, pred[32,128]{1,0:T(8,128)(4,1)S(1)} %compare_and_fusion, ...), kind=kOutput, calls=%fused_computation.55 | convolution fusion | flops 518160384 | bytes 42037328 | tf_op jit(solution)/shard_map/jvp(qkr,qc->krc)/dot_general | solution.py:41
  205.6 16.3 %gather_fusion = f32[4096,256]{1,0:T(8,128)} fusion(f32[192,256]{1,0:T(8,128)S(1)} %constant_dynamic-update-slice_fusion.9, s32[4096]{0:T(1024)S(1)} %copy-done.42), kind=kCustom, calls=%fused_computation.36 | custom fusion | bytes 8404992 | tf_op jit(solution)/shard_map/jvp(jvp(jit(_take)))/gather | solution.py:64
  222.0 16.2 %gather_fusion.1 = f32[4096,256]{1,0:T(8,128)} fusion(f32[192,256]{1,0:T(8,128)S(1)} %constant_dynamic-update-slice_fusion.18, s32[4096]{0:T(1024)S(1)} %copy-done.42), kind=kCustom, calls=%fused_computation.38 | custom fusion | bytes 8404992 | tf_op jit(solution)/shard_map/jvp(jvp(jit(_take)))/gather | solution.py:64
  238.3 11.9 %add_reduce_fusion.2 = (f32[128,256]{1,0:T(8,128)S(1)}, f32[128,256]{1,0:T(8,128)S(1)}, f32[32,128,256]{2,1,0:T(8,128)S(1)}) fusion(f32[32,128,256]{2,1,0:T(8,128)} %bitcast.229, f32[32,128,256]{2,1,0:T(8,128)} %bitcast.225, f32[32,128]{1,0:T(8,128)S(1)} %get-tuple-element.110, f32[32,128,256]{2,1,0:T(8,128)} %fusion.158, ...), kind=kOutput, calls=%fused_computation.73 | convolution fusion | flops 264339456 | bytes 17113168 | tf_op jit(solution)/shard_map/jvp(jvp(qkr,qc->krc))/dot_general | solution.py:41
  253.0 7.0 %multiply_reduce_fusion.1 = (f32[32,128]{1,0:T(8,128)}, f32[32,128]{1,0:T(8,128)}, f32[32,128,256]{2,1,0:T(8,128)}, f32[32,128,256]{2,1,0:T(8,128)}) fusion(f32[32,128,256]{2,1,0:T(8,128)S(1)} %get-tuple-element.216, f32[32,128,256]{2,1,0:T(8,128)S(1)} %bitcast.227, f32[128,256]{1,0:T(8,128)S(1)} %get-tuple-element.217, ...), kind=kLoop, calls=%fused_computation.78 | loop fusion | flops 20963328 | bytes 25497600 | tf_op jit(solution)/shard_map/jvp(transpose(jvp()))/reduce_sum | solution.py:42
  260.1 22.9 %scatter_custom_fusion.1 = f32[192,256]{1,0:T(8,128)S(1)} fusion(s32[4096]{0:T(1024)} %fusion.268, f32[4096,256]{1,0:T(8,128)} %bitcast.234, f32[]{:T(128)} %constant.71.clone.1), kind=kCustom, calls=%fused_computation.294 | custom fusion | flops 1048576 | bytes 197120 | tf_op jit(solution)/shard_map/jvp(transpose(jvp(jit(_take))))/scatter-add | solution.py:64
  283.7 22.9 %scatter_custom_fusion.6 = f32[192,256]{1,0:T(8,128)S(1)} fusion(s32[4096]{0:T(1024)} %fusion.268, f32[4096,256]{1,0:T(8,128)} %bitcast.233, f32[]{:T(128)} %constant.71.clone.1), kind=kCustom, calls=%fused_computation.292 | custom fusion | flops 1048576 | bytes 197120 | tf_op jit(solution)/shard_map/jvp(transpose(jvp(jit(_take))))/scatter-add | solution.py:64
  307.3 8.3 %fusion.7 = f32[32,128,20]{1,2,0:T(8,128)} fusion(f32[32,128,256]{2,1,0:T(8,128)} %bitcast.226, f32[32,128,256]{2,1,0:T(8,128)} %bitcast.230, f32[128,256]{1,0:T(8,128)S(1)} %get-tuple-element.219, f32[32,128]{1,0:T(8,128)S(1)} %get-tuple-element.110, f32[128,256]{1,0:T(8,128)S(1)} %get-tuple-element.217, f32[32,128]{1,0:T(8,128)S(1)} %get-tuple-element.133, ...), kind=kOutput, calls=%fused_computation.67 | convolution fusion | flops 261095424 | bytes 9035776 | tf_op jit(solution)/shard_map/jvp(transpose(jvp(qkr,qc->krc)))/dot_general | solution.py:41
  353.0 6.6 %fusion.16 = f32[128,3,32]{2,1,0:T(4,128)} fusion(f32[32,128,256]{2,1,0:T(8,128)S(1)} %copy-done.9, f32[128,256,3]{1,0,2:T(8,128)S(1)} %fusion.59), kind=kOutput, calls=%fused_computation.82 | convolution fusion | flops 37748736 | bytes 4636672 | tf_op jit(solution)/shard_map/jvp(transpose(jvp(ckr,krf->crf)))/dot_general | solution.py:51
  359.6 6.8 %fusion.62 = f32[3,32,128]{1,0,2:T(4,128)} fusion(f32[32,128,256]{2,1,0:T(8,128)S(1)} %copy-done.3, f32[128,256,3]{1,0,2:T(8,128)S(1)} %fusion.59), kind=kOutput, calls=%fused_computation.121 | convolution fusion | flops 37748736 | bytes 4636672 | tf_op jit(solution)/shard_map/jvp(transpose(jvp(ckr,krf->crf)))/dot_general | solution.py:51
  399.5 6.6 %fusion.6 = f32[32,128,256]{2,1,0:T(8,128)} fusion(f32[128,256,32]{1,2,0:T(8,128)S(1)} %copy-done.12, f32[128,256,32]{1,2,0:T(8,128)S(1)} %fusion.90), kind=kLoop, calls=%fused_computation.64 | loop fusion | flops 1048576 | bytes 12582912 | tf_op jit(solution)/shard_map/jvp(transpose(jvp(ckr,krf->crf)))/add_any | solution.py:51
  416.2 12.6 %fusion = f32[32,128,20]{1,2,0:T(8,128)S(1)} fusion(f32[32,128,512]{2,1,0:T(8,128)S(1)} %add_multiply_fusion.2, f32[32,128]{1,0:T(8,128)S(1)} %copy-done.53, f32[32,128]{1,0:T(8,128)S(1)} %copy-done.40, f32[32,128,256]{2,1,0:T(8,128)} %broadcast_in_dim.163, f32[32,128,256]{2,1,0:T(8,128)} %fusion.6, f32[32,128,512]{2,1,0:T(8,128)S(1)} %bitcast.224, ...), kind=kOutput, calls=%fused_computation.49 | convolution fusion | flops 515899392 | bytes 25571328 | tf_op jit(solution)/shard_map/jvp(transpose(jvp(qkr,qc->krc)))/dot_general | solution.py:41
  429.0 10.6 %fusion.97 = (f32[32,128]{1,0:T(8,128)S(1)}, f32[32,128]{1,0:T(8,128)S(1)}, f32[32,128]{1,0:T(8,128)S(1)}, f32[32,128]{1,0:T(8,128)S(1)}, f32[32,128]{1,0:T(8,12...) fusion(f32[32,128,20]{1,2,0:T(8,128)S(1)} %fusion, f32[32,128]{1,0:T(8,128)S(1)} %copy-done.71, ...), kind=kOutput, calls=%fused_computation.156 | convolution fusion | flops 509558784 | bytes 9642064 | tf_op jit(solution)/shard_map/jvp(transpose(jvp(qkr,qc->krc)))/dot_general | solution.py:41
  443.9 22.7 %scatter_fusion = f32[3,192]{0,1:T(8,128)S(1)} fusion(f32[3,192]{0,1:T(8,128)S(1)} %pad.24, s32[4096]{0:T(1024)S(1)} %copy-done.54, f32[4096,3]{1,0:T(8,128)} %bitcast.239), kind=kCustom, calls=%fused_computation.39 | custom fusion | flops 12288 | bytes 163840 | tf_op jit(solution)/shard_map/jvp(transpose(jvp(jit(_take))))/scatter-add | solution.py:28
  469.6 22.7 %scatter_fusion.2 = f32[3,192]{0,1:T(8,128)S(1)} fusion(f32[3,192]{0,1:T(8,128)S(1)} %pad.28, s32[4096]{0:T(1024)S(1)} %copy-done.54, f32[4096,3]{1,0:T(8,128)} %bitcast.240), kind=kCustom, calls=%fused_computation.43 | custom fusion | flops 12288 | bytes 163840 | tf_op jit(solution)/shard_map/jvp(transpose(jvp(jit(_take))))/scatter-add | solution.py:28
  501.0 14.3 %multiply_reduce_fusion = (f32[32,128]{1,0:T(8,128)S(1)}, f32[32,128]{1,0:T(8,128)S(1)}) fusion(f32[32,128,512]{2,1,0:T(8,128)} %get-tuple-element.210, f32[32,128,512]{2,1,0:T(8,128)} %copy-done.5, f32[32,128,256]{2,1,0:T(8,128)} %broadcast_in_dim.163, f32[32,128,256]{2,1,0:T(8,128)} %fusion.6, f32[32,128,512]{2,1,0:T(8,128)} %bitcast.221, ...), kind=kLoop, calls=%fused_computation.58 | loop fusion | flops 18866176 | bytes 41979904 | tf_op jit(solution)/shard_map/jvp(transpose(jvp()))/reduce_sum | solution.py:42
  520.7 22.4 %scatter_fusion.1 = f32[3,192]{0,1:T(8,128)S(1)} fusion(f32[3,192]{0,1:T(8,128)S(1)} %pad.27, s32[4096]{0:T(1024)S(1)} %copy-done.54, f32[4096,3]{1,0:T(8,128)S(1)} %bitcast.236), kind=kCustom, calls=%fused_computation.42 | custom fusion | flops 12288 | bytes 163840 | tf_op jit(solution)/shard_map/jvp(transpose(jvp(jit(_take))))/scatter-add | solution.py:28
  545.2 22.4 %scatter_fusion.3 = f32[3,192]{0,1:T(8,128)S(1)} fusion(f32[3,192]{0,1:T(8,128)S(1)} %pad.31, s32[4096]{0:T(1024)S(1)} %copy-done.54, f32[4096,3]{1,0:T(8,128)S(1)} %bitcast.235), kind=kCustom, calls=%fused_computation.47 | custom fusion | flops 12288 | bytes 163840 | tf_op jit(solution)/shard_map/jvp(transpose(jvp(jit(_take))))/scatter-add | solution.py:28
  (527 shorter events, 249.1 us)
Async XLA Ops:
  5.5 76.0 %collective-permute-start.5 = (f32[24,512]{1,0:T(8,128)S(1)}, f32[24,512]{1,0:T(8,128)S(1)}, u32[]{:S(2)}, u32[]{:S(2)}) collective-permute-start(f32[24,512]{1,0:T(8,128)S(1)} %pad_maximum_fusion.1), channel_id=1, source_target_pairs={{8,0},{16,8},{24,16},{9,1},{17,9},{25,17},{10,2},{18,10},{26,18},{... | collective-permute-start | bytes 147464 | tf_op jit(solution)/shard_map/ppermute | solution.py:17
  8.7 72.8 %collective-permute-start.4 = (f32[24,512]{1,0:T(8,128)S(1)}, f32[24,512]{1,0:T(8,128)S(1)}, u32[]{:S(2)}, u32[]{:S(2)}) collective-permute-start(f32[24,512]{1,0:T(8,128)S(1)} %pad_maximum_fusion), channel_id=1, source_target_pairs={{0,8},{8,16},{16,24},{1,9},{9,17},{17,25},{2,10},{10,18},{18,26},{... | collective-permute-start | bytes 147464 | tf_op jit(solution)/shard_map/ppermute | solution.py:17
  16.8 15.9 %collective-permute-start = (f32[24,6]{0,1:T(8,128)S(1)}, f32[24,6]{0,1:T(8,128)S(1)}, u32[]{:S(2)}, u32[]{:S(2)}) collective-permute-start(f32[24,6]{0,1:T(8,128)S(1)} %pad_maximum_fusion.21), channel_id=1, source_target_pairs={{0,8},{8,16},{16,24},{1,9},{9,17},{17,25},{2,10},{10,18},{18,26},{... | collective-permute-start | bytes 1736 | tf_op jit(solution)/shard_map/ppermute | solution.py:17
  21.8 11.0 %collective-permute-start.1 = (f32[24,6]{0,1:T(8,128)S(1)}, f32[24,6]{0,1:T(8,128)S(1)}, u32[]{:S(2)}, u32[]{:S(2)}) collective-permute-start(f32[24,6]{0,1:T(8,128)S(1)} %pad_maximum_fusion.22), channel_id=1, source_target_pairs={{8,0},{16,8},{24,16},{9,1},{17,9},{25,17},{10,2},{18,10},{26,18},{... | collective-permute-start | bytes 1736 | tf_op jit(solution)/shard_map/ppermute | solution.py:17
  81.5 21.1 %collective-permute-start.6 = (f32[24,512]{1,0:T(8,128)S(1)}, f32[24,512]{1,0:T(8,128)S(1)}, u32[]{:S(2)}, u32[]{:S(2)}) collective-permute-start(f32[24,512]{1,0:T(8,128)S(1)} %pad_maximum_fusion.2), channel_id=1, source_target_pairs={{0,1},{1,2},{2,3},{3,4},{4,5},{5,6},{6,7},{8,9},{9,10},{10,11},{11... | collective-permute-start | bytes 147464 | tf_op jit(solution)/shard_map/ppermute | solution.py:17
  178.6 15.9 %collective-permute-start.9 = (f32[24,256]{1,0:T(8,128)S(1)}, f32[24,256]{1,0:T(8,128)S(1)}, u32[]{:S(2)}, u32[]{:S(2)}) collective-permute-start(f32[24,256]{1,0:T(8,128)S(1)} %pad_maximum_fusion.5), channel_id=1, source_target_pairs={{8,0},{16,8},{24,16},{9,1},{17,9},{25,17},{10,2},{18,10},{26,18},{... | collective-permute-start | bytes 73736 | tf_op jit(solution)/shard_map/ppermute | solution.py:17
  182.1 12.4 %collective-permute-start.8 = (f32[24,256]{1,0:T(8,128)S(1)}, f32[24,256]{1,0:T(8,128)S(1)}, u32[]{:S(2)}, u32[]{:S(2)}) collective-permute-start(f32[24,256]{1,0:T(8,128)S(1)} %pad_maximum_fusion.4), channel_id=1, source_target_pairs={{0,8},{8,16},{16,24},{1,9},{9,17},{17,25},{2,10},{10,18},{18,26},{... | collective-permute-start | bytes 73736 | tf_op jit(solution)/shard_map/ppermute | solution.py:17
  187.3 9.2 %collective-permute-start.17 = (f32[24,256]{1,0:T(8,128)S(1)}, f32[24,256]{1,0:T(8,128)S(1)}, u32[]{:S(2)}, u32[]{:S(2)}) collective-permute-start(f32[24,256]{1,0:T(8,128)S(1)} %pad_maximum_fusion.13), channel_id=1, source_target_pairs={{8,0},{16,8},{24,16},{9,1},{17,9},{25,17},{10,2},{18,10},{26,18},{... | collective-permute-start | bytes 73736 | tf_op jit(solution)/shard_map/ppermute | solution.py:17
  188.6 7.9 %collective-permute-start.16 = (f32[24,256]{1,0:T(8,128)S(1)}, f32[24,256]{1,0:T(8,128)S(1)}, u32[]{:S(2)}, u32[]{:S(2)}) collective-permute-start(f32[24,256]{1,0:T(8,128)S(1)} %pad_maximum_fusion.12), channel_id=1, source_target_pairs={{0,8},{8,16},{16,24},{1,9},{9,17},{17,25},{2,10},{10,18},{18,26},{... | collective-permute-start | bytes 73736 | tf_op jit(solution)/shard_map/ppermute | solution.py:17
  203.1 18.8 %collective-permute-start.19 = (f32[24,256]{1,0:T(8,128)S(1)}, f32[24,256]{1,0:T(8,128)S(1)}, u32[]{:S(2)}, u32[]{:S(2)}) collective-permute-start(f32[24,256]{1,0:T(8,128)S(1)} %pad_maximum_fusion.15), channel_id=1, source_target_pairs={{1,0},{2,1},{3,2},{4,3},{5,4},{6,5},{7,6},{9,8},{10,9},{11,10},{12... | collective-permute-start | bytes 73736 | tf_op jit(solution)/shard_map/ppermute | solution.py:17
  320.7 13.0 %collective-permute-start.12 = (f32[24,256]{1,0:T(8,128)S(1)}, f32[24,256]{1,0:T(8,128)S(1)}, u32[]{:S(2)}, u32[]{:S(2)}) collective-permute-start(f32[24,256]{1,0:T(8,128)S(1)} %pad_maximum_fusion.8), channel_id=1, source_target_pairs={{0,1},{1,2},{2,3},{3,4},{4,5},{5,6},{6,7},{8,9},{9,10},{10,11},{11... | collective-permute-start | bytes 73736 | tf_op jit(solution)/shard_map/ppermute | solution.py:17
  322.7 11.1 %collective-permute-start.13 = (f32[24,256]{1,0:T(8,128)S(1)}, f32[24,256]{1,0:T(8,128)S(1)}, u32[]{:S(2)}, u32[]{:S(2)}) collective-permute-start(f32[24,256]{1,0:T(8,128)S(1)} %pad_maximum_fusion.9), channel_id=1, source_target_pairs={{1,0},{2,1},{3,2},{4,3},{5,4},{6,5},{7,6},{9,8},{10,9},{11,10},{12... | collective-permute-start | bytes 73736 | tf_op jit(solution)/shard_map/ppermute | solution.py:17
  327.2 11.8 %collective-permute-start.24 = (f32[24,256]{1,0:T(8,128)S(1)}, f32[24,256]{1,0:T(8,128)S(1)}, u32[]{:S(2)}, u32[]{:S(2)}) collective-permute-start(f32[24,256]{1,0:T(8,128)S(1)} %pad_maximum_fusion.16), channel_id=1, source_target_pairs={{0,1},{1,2},{2,3},{3,4},{4,5},{5,6},{6,7},{8,9},{9,10},{10,11},{11... | collective-permute-start | bytes 73736 | tf_op jit(solution)/shard_map/ppermute | solution.py:17
  329.2 9.9 %collective-permute-start.25 = (f32[24,256]{1,0:T(8,128)S(1)}, f32[24,256]{1,0:T(8,128)S(1)}, u32[]{:S(2)}, u32[]{:S(2)}) collective-permute-start(f32[24,256]{1,0:T(8,128)S(1)} %pad_maximum_fusion.17), channel_id=1, source_target_pairs={{1,0},{2,1},{3,2},{4,3},{5,4},{6,5},{7,6},{9,8},{10,9},{11,10},{12... | collective-permute-start | bytes 73736 | tf_op jit(solution)/shard_map/ppermute | solution.py:17
  333.8 12.9 %collective-permute-start.14 = (f32[24,256]{1,0:T(8,128)S(1)}, f32[24,256]{1,0:T(8,128)S(1)}, u32[]{:S(2)}, u32[]{:S(2)}) collective-permute-start(f32[24,256]{1,0:T(8,128)S(1)} %pad_maximum_fusion.10), channel_id=1, source_target_pairs={{0,8},{8,16},{16,24},{1,9},{9,17},{17,25},{2,10},{10,18},{18,26},{... | collective-permute-start | bytes 73736 | tf_op jit(solution)/shard_map/ppermute | solution.py:17
  337.7 9.0 %collective-permute-start.15 = (f32[24,256]{1,0:T(8,128)S(1)}, f32[24,256]{1,0:T(8,128)S(1)}, u32[]{:S(2)}, u32[]{:S(2)}) collective-permute-start(f32[24,256]{1,0:T(8,128)S(1)} %pad_maximum_fusion.11), channel_id=1, source_target_pairs={{8,0},{16,8},{24,16},{9,1},{17,9},{25,17},{10,2},{18,10},{26,18},{... | collective-permute-start | bytes 73736 | tf_op jit(solution)/shard_map/ppermute | solution.py:17
  339.7 36.9 %collective-permute-start.26 = (f32[24,256]{1,0:T(8,128)}, f32[24,256]{1,0:T(8,128)}, u32[]{:S(2)}, u32[]{:S(2)}) collective-permute-start(f32[24,256]{1,0:T(8,128)} %pad_maximum_fusion.18), channel_id=1, source_target_pairs={{0,8},{8,16},{16,24},{1,9},{9,17},{17,25},{2,10},{10,18},{18,26},{... | collective-permute-start | bytes 73736 | tf_op jit(solution)/shard_map/ppermute | solution.py:17
  345.4 31.1 %collective-permute-start.27 = (f32[24,256]{1,0:T(8,128)}, f32[24,256]{1,0:T(8,128)S(1)}, u32[]{:S(2)}, u32[]{:S(2)}) collective-permute-start(f32[24,256]{1,0:T(8,128)} %pad_maximum_fusion.19), channel_id=1, source_target_pairs={{8,0},{16,8},{24,16},{9,1},{17,9},{25,17},{10,2},{18,10},{26,18},{... | collective-permute-start | bytes 73736 | tf_op jit(solution)/shard_map/ppermute | solution.py:17
  493.8 80.7 %collective-permute-start.20 = (f32[24,6]{0,1:T(8,128)}, f32[24,6]{0,1:T(8,128)}, u32[]{:S(2)}, u32[]{:S(2)}) collective-permute-start(f32[24,6]{0,1:T(8,128)} %pad_maximum_fusion.28), channel_id=1, source_target_pairs={{0,1},{1,2},{2,3},{3,4},{4,5},{5,6},{6,7},{8,9},{9,10},{10,11},{11... | collective-permute-start | bytes 1736 | tf_op jit(solution)/shard_map/ppermute | solution.py:17
  496.4 78.9 %collective-permute-start.21 = (f32[24,6]{0,1:T(8,128)}, f32[24,6]{0,1:T(8,128)S(1)}, u32[]{:S(2)}, u32[]{:S(2)}) collective-permute-start(f32[24,6]{0,1:T(8,128)} %pad_maximum_fusion.29), channel_id=1, source_target_pairs={{1,0},{2,1},{3,2},{4,3},{5,4},{6,5},{7,6},{9,8},{10,9},{11,10},{12... | collective-permute-start | bytes 1736 | tf_op jit(solution)/shard_map/ppermute | solution.py:17
  567.9 13.5 %collective-permute-start.28 = (f32[24,6]{0,1:T(8,128)S(1)}, f32[24,6]{0,1:T(8,128)S(1)}, u32[]{:S(2)}, u32[]{:S(2)}) collective-permute-start(f32[24,6]{0,1:T(8,128)S(1)} %pad_maximum_fusion.34), channel_id=1, source_target_pairs={{0,1},{1,2},{2,3},{3,4},{4,5},{5,6},{6,7},{8,9},{9,10},{10,11},{11... | collective-permute-start | bytes 1736 | tf_op jit(solution)/shard_map/ppermute | solution.py:17
  569.9 11.6 %collective-permute-start.29 = (f32[24,6]{0,1:T(8,128)S(1)}, f32[24,6]{0,1:T(8,128)S(1)}, u32[]{:S(2)}, u32[]{:S(2)}) collective-permute-start(f32[24,6]{0,1:T(8,128)S(1)} %pad_maximum_fusion.35), channel_id=1, source_target_pairs={{1,0},{2,1},{3,2},{4,3},{5,4},{6,5},{7,6},{9,8},{10,9},{11,10},{12... | collective-permute-start | bytes 1736 | tf_op jit(solution)/shard_map/ppermute | solution.py:17
  575.5 12.1 %collective-permute-start.22 = (f32[24,6]{0,1:T(8,128)S(1)}, f32[24,6]{0,1:T(8,128)S(1)}, u32[]{:S(2)}, u32[]{:S(2)}) collective-permute-start(f32[24,6]{0,1:T(8,128)S(1)} %pad_maximum_fusion.30), channel_id=1, source_target_pairs={{0,8},{8,16},{16,24},{1,9},{9,17},{17,25},{2,10},{10,18},{18,26},{... | collective-permute-start | bytes 1736 | tf_op jit(solution)/shard_map/ppermute | solution.py:17
  580.1 7.5 %collective-permute-start.23 = (f32[24,6]{0,1:T(8,128)S(1)}, f32[24,6]{0,1:T(8,128)S(1)}, u32[]{:S(2)}, u32[]{:S(2)}) collective-permute-start(f32[24,6]{0,1:T(8,128)S(1)} %pad_maximum_fusion.31), channel_id=1, source_target_pairs={{8,0},{16,8},{24,16},{9,1},{17,9},{25,17},{10,2},{18,10},{26,18},{... | collective-permute-start | bytes 1736 | tf_op jit(solution)/shard_map/ppermute | solution.py:17
  (113 other events, 2341.1 us)
where the time goes:
time: 604 us; the launch traced here: 595 us
  other arithmetic  196 us (32%)
  matrix products  147 us (24%)
  local copies, waits for them, and re-layouts  134 us (22%)
  starting transfers between devices  104 us (17%)
  waiting for transfers between devices  9.3 us (2%)
    ppermute x32, starting transfers between devices, passed_along(): return lax.ppermute(block, axis, route)  104 us
    scatter-add x4, other arithmetic, geometry(): others = jnp.take(pos_table, own_lists, axis=1)  90.3 us
    dot_general x8, matrix products, edge_weights(): mixed = jnp.einsum('qkr,qc->krc', radial, filter_table, precision=highest)  80.4 us
    dot_general x9, matrix products, first_layer(): jnp.einsum('ckr,krf->crf', direction, message[:, :, channels:], precision...  47.7 us
    scatter-add x2, other arithmetic, second_layer(): jnp.take(phi_table, own_lists, axis=0)  45.8 us
    gather x2, local copies, waits for them, and re-layouts, second_layer(): jnp.take(phi_table, own_lists, axis=0)  32.5 us
    gather x4, local copies, waits for them, and re-layouts, geometry(): others = jnp.take(pos_table, own_lists, axis=1)  28.9 us
    gather x32, local copies, waits for them, and re-layouts, toward(): return tuple((jnp.take(member, chosen, axis=0) for member in payload))  23.7 us
  transfers between devices with their start and end apart: 32, of which 4 were waited for; matrix products, arithmetic and copies ran while one was open for 31% of the time, Pallas kernels for 0%

commit v1 on v0

v1 whole, which is shorter than its diff:
```python
import functools
import math

import jax
import jax.numpy as jnp
from jax import lax
from jax.experimental import pallas as pl
from jax.experimental.pallas import tpu as pltpu
from jax.sharding import PartitionSpec as P

f32 = jnp.float32
bf16 = jnp.bfloat16
cutoff_radius = 3.0
softening = 0.01
wave = math.pi / cutoff_radius
offsets = ((-1, -1), (-1, 0), (-1, 1), (0, -1), (0, 1), (1, -1), (1, 0), (1, 1))
lanes = 128
wide = 256
row_block = 32
nn_dims = (((1,), (0,)), ((), ()))
nt_dims = (((1,), (1,)), ((), ()))

U, UD, DD, P0, P1, P2, SN, CS, RS, RC, RI = 0, 3, 6, 7, 8, 9, 10, 11, 12, 13, 14
geo_slots = 15


def split(value):
    high = value.astype(bf16)
    return high, (value - high.astype(f32)).astype(bf16)


def mxu(left, right, dims=nn_dims):
    return lax.dot_general(left, right, dims, preferred_element_type=f32)


def dot3(left, right, dims=nn_dims):
    lh, ll = split(left)
    rh, rl = split(right)
    return mxu(lh, rh, dims) + mxu(ll, rh, dims) + mxu(lh, rl, dims)


def sigmoid(value):
    return 1.0 / (1.0 + jnp.exp(-jnp.maximum(value, -80.0)))


def silu_parts(value):
    gate = sigmoid(value)
    first = gate * (1.0 + value * (1.0 - gate))
    second = gate * (1.0 - gate) * (2.0 + value * (1.0 - 2.0 * gate))
    return value * gate, first, second


def sin_cos(theta):
    t = jnp.minimum(theta, 6.0) * 0.25
    x = t * t
    s = -1.0 / 39916800.0 + x * (1.0 / 6227020800.0)
    s = 1.0 / 362880.0 + x * s
    s = -1.0 / 5040.0 + x * s
    s = 1.0 / 120.0 + x * s
    s = -1.0 / 6.0 + x * s
    s = t + t * x * s
    c = 1.0 / 479001600.0 - x * (1.0 / 87178291200.0)
    c = -1.0 / 3628800.0 + x * c
    c = 1.0 / 40320.0 + x * c
    c = -1.0 / 720.0 + x * c
    c = 1.0 / 24.0 + x * c
    c = -0.5 + x * c
    c = 1.0 + x * c
    s, c = 2.0 * s * c, 1.0 - 2.0 * s * s
    return 2.0 * s * c, 1.0 - 2.0 * s * s


def fill_geometry(geo, first, second, mask_at, height, members):
    repeats = wide // members
    group = lax.broadcasted_iota(jnp.int32, (1, wide), 1) // members
    for start in range(0, height, row_block):
        rows = pl.ds(start, row_block)
        off = [first(i, start) - second(i, start) for i in range(3)]
        move = [first(i + 3, start) - second(i + 3, start) for i in range(3)]
        square = off[0] * off[0] + off[1] * off[1] + off[2] * off[2] + softening
        inverse = lax.rsqrt(square)
        inverse = inverse * (1.5 - 0.5 * square * inverse * inverse)
        theta = wave * (square * inverse)
        unit = [o * inverse for o in off]
        speed = unit[0] * move[0] + unit[1] * move[1] + unit[2] * move[2]
        for i in range(3):
            geo[U + i, rows, :] = unit[i]
            geo[UD + i, rows, :] = (move[i] - unit[i] * speed) * inverse
        sn, cs = sin_cos(theta)
        g0 = (0.5 * cs + 0.5) * inverse
        g1 = ((-0.5 * wave) * sn - g0) * inverse
        g2 = ((-0.5 * wave * wave) * cs - 2.0 * g1) * inverse
        mask = mask_at(start)
        geo[DD, rows, :] = speed
        geo[P0, rows, :] = mask * g0
        geo[P1, rows, :] = mask * g1
        geo[P2, rows, :] = mask * g2
        geo[RI, rows, :] = inverse
        turn_s, turn_c = sn, cs
        state_s, state_c = sn, cs
        for i in range(1, repeats):
            turn_s, turn_c = turn_s * cs + turn_c * sn, turn_c * cs - turn_s * sn
            state_s = jnp.where(group >= i, turn_s, state_s)
            state_c = jnp.where(group >= i, turn_c, state_c)
        geo[SN, rows, :] = state_s
        geo[CS, rows, :] = state_c
        geo[RS, rows, :] = turn_s
        geo[RC, rows, :] = turn_c


def order_factor(step, members):
    repeats = wide // members
    group = lax.broadcasted_iota(jnp.int32, (1, wide), 1) // members
    return (group + (step * repeats + 1)).astype(f32) * wave


def rotate(geo, rows, s, c):
    rs = geo[RS, rows, :]
    rc = geo[RC, rows, :]
    geo[SN, rows, :] = s * rc + c * rs
    geo[CS, rows, :] = c * rc - s * rs


def listed(nbr_ref, start, members):
    slot = lax.broadcasted_iota(jnp.int32, (members, lanes), 0) + start
    found = nbr_ref[0:1, :] == slot
    for k in range(1, nbr_ref.shape[0]):
        found = found | (nbr_ref[k : k + 1, :] == slot)
    return jnp.where(found, 1.0, 0.0).astype(f32)


def stack_coords(box, pos_ref, tan_ref):
    box[...] = jnp.zeros_like(box)
    box[0:3, :] = pos_ref[...]
    box[3:6, :] = tan_ref[...]


def geometry_by_atom(geo, box, wbox, ghost_ref, nbr_ref, own_rows, ghost):
    columns = box[...].T
    if ghost:
        members = ghost_ref.shape[0]
        repeats = wide // members
        table = jnp.concatenate([ghost_ref[...]] * repeats, 0).T
        mask = listed(nbr_ref, own_rows, members)
    else:
        members = own_rows
        repeats = wide // members
        table = jnp.concatenate([box[...]] * repeats, 1)
        mask = listed(nbr_ref, 0, members)
    wbox[...] = jnp.concatenate([mask] * repeats, 0).T
    fill_geometry(
        geo,
        lambda i, start: table[i : i + 1, :],
        lambda i, start: columns[start : start + row_block, i : i + 1],
        lambda start: wbox[start : start + row_block, :],
        own_rows,
        members,
    )
    return members


def geometry_by_slot(geo, box, wbox, ghost_ref, nbr_ref, own_rows, ghost):
    repeats = wide // own_rows
    centre = jnp.concatenate([box[...]] * repeats, 1)
    if ghost:
        height = ghost_ref.shape[0]
        columns = ghost_ref[...]
        mask = listed(nbr_ref, own_rows, height)
    else:
        height = own_rows
        columns = box[...].T
        mask = listed(nbr_ref, 0, height)
    wbox[0:height, :] = jnp.concatenate([mask] * repeats, 1)
    fill_geometry(
        geo,
        lambda i, start: columns[start : start + row_block, i : i + 1],
        lambda i, start: centre[i : i + 1, :],
        lambda start: wbox[start : start + row_block, :],
        height,
        own_rows,
    )
    return height


def scaled_rows(high, low, filter_ref, value, step, columns, scale):
    members = value.shape[0]
    for i in range(wide // members):
        row = filter_ref[pl.ds(step * (wide // members) + i, 1), columns] * scale
        h, l = split(row * value)
        high[i * members : (i + 1) * members, :] = h
        low[i * members : (i + 1) * members, :] = l


def put_split(high, low, start, value):
    h, l = split(value)
    high[start : start + value.shape[0], :] = h
    low[start : start + value.shape[0], :] = l


def first_messages(acc, geo, ah, al, gh, gl, vh, vl, phi_ref, filter_ref, members, scale, fresh):
    height = geo.shape[1]
    channels = phi_ref.shape[1] // 2
    if fresh:
        acc[...] = jnp.zeros_like(acc)

    def chunk(step, _):
        factor = order_factor(step, members)
        scaled_rows(gh, gl, filter_ref, phi_ref[:, :channels], step, slice(0, channels), scale)
        scaled_rows(
            vh, vl, filter_ref, phi_ref[:, channels:], step, slice(channels, 2 * channels), scale
        )
        for start in range(0, height, row_block):
            rows = pl.ds(start, row_block)
            s, c = geo[SN, rows, :], geo[CS, rows, :]
            p0 = geo[P0, rows, :]
            b = p0 * s
            bd = (geo[P1, rows, :] * s + factor * (p0 * c)) * geo[DD, rows, :]
            put_split(ah, al, start, b)
            put_split(ah, al, height + start, bd)
            for i in range(3):
                unit = geo[U + i, rows, :]
                put_split(ah, al, (2 + i) * height + start, unit * b)
                put_split(ah, al, (5 + i) * height + start, geo[UD + i, rows, :] * b + unit * bd)
            rotate(geo, rows, s, c)
        top = 2 * height
        acc[:top, :] += (
            mxu(ah[:top, :], gh[...]) + mxu(al[:top, :], gh[...]) + mxu(ah[:top, :], gl[...])
        )
        acc[top:, :] += (
            mxu(ah[top:, :], vh[...]) + mxu(al[top:, :], vh[...]) + mxu(ah[top:, :], vl[...])
        )
        return 0

    lax.fori_loop(0, filter_ref.shape[0] * members // wide, chunk, 0)


def second_messages(acc, geo, ah, al, gh, gl, vh, vl, value, dots, filter_ref, members, scale):
    height = acc.shape[0] // 2

    def chunk(step, _):
        factor = order_factor(step, members)
        scaled_rows(gh, gl, filter_ref, value(), step, slice(None), scale)
        scaled_rows(vh, vl, filter_ref, dots(), step, slice(None), scale)
        for start in range(0, height, row_block):
            rows = pl.ds(start, row_block)
            s, c = geo[SN, rows, :], geo[CS, rows, :]
            p0 = geo[P0, rows, :]
            put_split(ah, al, start, p0 * s)
            put_split(
                ah,
                al,
                height + start,
                (geo[P1, rows, :] * s + factor * (p0 * c)) * geo[DD, rows, :],
            )
            rotate(geo, rows, s, c)
        top = 2 * height
        acc[...] += (
            mxu(ah[:top, :], gh[...]) + mxu(al[:top, :], gh[...]) + mxu(ah[:top, :], gl[...])
        )
        acc[height:, :] += (
            mxu(ah[:height, :], vh[...])
            + mxu(al[:height, :], vh[...])
            + mxu(ah[:height, :], vl[...])
        )
        return 0

    lax.fori_loop(0, filter_ref.shape[0] * members // wide, chunk, 0)


def neighbour_id(target, sizes):
    along = lax.axis_index("bx") + target[0]
    across = lax.axis_index("by") + target[1]
    inside = (along >= 0) & (along < sizes[0]) & (across >= 0) & (across < sizes[1])
    device = jnp.clip(along, 0, sizes[0] - 1) * sizes[1] + jnp.clip(across, 0, sizes[1] - 1)
    return device, inside


def send_gathered(out_ref, table, send_ref, sizes):
    count = out_ref.shape[1]
    for number, target in enumerate(offsets):
        device, inside = neighbour_id(target, sizes)

        @pl.when(inside)
        def _():
            for p in range(count):
                index = send_ref[0, number * count + p]
                out_ref[device, p : p + 1, :] = table[pl.ds(index, 1), :]


def send_groups(out_ref, table, sizes):
    count = out_ref.shape[1]
    for number, target in enumerate(offsets):
        device, inside = neighbour_id(target, sizes)

        @pl.when(inside)
        def _():
            out_ref[device] = table[number * count : (number + 1) * count, :]


def receive_groups(table, in_ref, sizes):
    count = in_ref.shape[1]
    table[...] = jnp.zeros_like(table)
    for number, target in enumerate(offsets):
        device, inside = neighbour_id(target, sizes)

        @pl.when(inside)
        def _():
            table[number * count : (number + 1) * count, :] = in_ref[device]


def add_returned(table, in_ref, send_ref, sizes):
    count = in_ref.shape[1]
    for number, target in enumerate(offsets):
        device, inside = neighbour_id(target, sizes)

        @pl.when(inside)
        def _():
            for p in range(count):
                index = send_ref[0, number * count + p]
                table[pl.ds(index, 1), :] += in_ref[device, p : p + 1, :]


def pack_kernel(sizes, pos, tan, emb, send, out, box, table):
    channels = emb.shape[1]
    stack_coords(box, pos, tan)
    table[:, :channels] = emb[...]
    table[:, channels:] = box[...].T
    send_gathered(out, table, send, sizes)


def first_own_kernel(
    scale, pos, tan, emb, nbr, w_in, w_out, filt, acc, phi, box, wbox, geo, ah, al, gh, gl, vh, vl
):
    stack_coords(box, pos, tan)
    phi[...] = dot3(silu_parts(dot3(emb[...], w_in[...]))[0], w_out[...])
    members = geometry_by_atom(geo, box, wbox, None, nbr, pos.shape[1], False)
    first_messages(acc, geo, ah, al, gh, gl, vh, vl, phi, filt, members, scale, True)


def first_ghost_kernel(
    sizes,
    scale,
    pos,
    tan,
    emb,
    nbr,
    send,
    w_in,
    w_out,
    filt,
    w_left,
    w_right,
    w_two_in,
    w_two_out,
    partial,
    arrived,
    out,
    state,
    inner,
    maps,
    phi_two,
    phi_ghost,
    coords_ghost,
    box,
    wbox,
    geo,
    ah,
    al,
    gh,
    gl,
    vh,
    vl,
    acc,
    table,
):
    own_rows = pos.shape[1]
    channels = emb.shape[1]
    stack_coords(box, pos, tan)
    receive_groups(table, arrived, sizes)
    coords_ghost[...] = table[:, channels:]
    phi_ghost[...] = dot3(silu_parts(dot3(table[:, :channels], w_in[...]))[0], w_out[...])
    members = geometry_by_atom(geo, box, wbox, coords_ghost, nbr, own_rows, True)
    acc[...] = partial[...]
    first_messages(acc, geo, ah, al, gh, gl, vh, vl, phi_ghost, filt, members, scale, False)
    top = 2 * own_rows
    half = 3 * own_rows
    maps[0 : 2 * half, :] = dot3(acc[top:, :], w_left[...])
    maps[2 * half :, :] = dot3(acc[top:, :], w_right[...])
    total = emb[...] + acc[0:own_rows, :]
    moved = acc[own_rows:top, :]
    for i in range(3):
        a, b = i * own_rows, (i + 1) * own_rows
        left, left_dot = maps[a:b, :], maps[half + a : half + b, :]
        right = maps[2 * half + a : 2 * half + b, :]
        right_dot = maps[3 * half + a : 3 * half + b, :]
        total = total + left * right
        moved = moved + left_dot * right + left * right_dot
    state[0:own_rows, :] = total
    state[own_rows:, :] = moved
    inner[...] = dot3(state[...], w_two_in[...])
    value, slope, _ = silu_parts(inner[0:own_rows, :])
    state_two = jnp.concatenate([value, slope * inner[own_rows:, :]], 0)
    outer = dot3(state_two, w_two_out[...])
    phi_two[:, :channels] = outer[:own_rows]
    phi_two[:, channels:] = outer[own_rows:]
    send_gathered(out, phi_two, send, sizes)


def second_own_kernel(
    scale, pos, tan, nbr, filt, phi_two, acc, box, wbox, geo, ah, al, gh, gl, vh, vl
):
    channels = filt.shape[1]
    stack_coords(box, pos, tan)
    members = geometry_by_atom(geo, box, wbox, None, nbr, pos.shape[1], False)
    acc[...] = jnp.zeros_like(acc)
    second_messages(
        acc,
        geo,
        ah,
        al,
        gh,
        gl,
        vh,
        vl,
        lambda: phi_two[:, :channels],
        lambda: phi_two[:, channels:],
        filt,
        members,
        scale,
    )


def second_ghost_kernel(
    sizes,
    scale,
    pos,
    tan,
    nbr,
    counts,
    filt,
    coords_ghost,
    state,
    partial,
    w_hidden,
    w_energy,
    arrived,
    out,
    table,
    cot,
    box,
    wbox,
    geo,
    ah,
    al,
    gh,
    gl,
    vh,
    vl,
    acc,
    back,
):
    own_rows = pos.shape[1]
    channels = filt.shape[1]
    stack_coords(box, pos, tan)
    receive_groups(table, arrived, sizes)
    members = geometry_by_atom(geo, box, wbox, coords_ghost, nbr, own_rows, True)
    acc[...] = partial[...]
    second_messages(
        acc,
        geo,
        ah,
        al,
        gh,
        gl,
        vh,
        vl,
        lambda: table[:, :channels],
        lambda: table[:, channels:],
        filt,
        members,
        scale,
    )
    hidden = dot3(state[...] + acc[...], w_hidden[...])
    _, slope, bend = silu_parts(hidden[:own_rows])
    live = lax.broadcasted_iota(jnp.int32, (own_rows, 1), 0) < counts[0]
    weight = jnp.where(live, w_energy[...], 0.0)
    bars = jnp.concatenate([weight * slope, weight * bend * hidden[own_rows:]], 0)
    cot[...] = dot3(bars, w_hidden[...], nt_dims)
    height = geometry_by_slot(geo, box, wbox, coords_ghost, nbr, own_rows, True)
    table_cotangents(back, geo, ah, al, gh, gl, vh, vl, cot, filt, height, own_rows, scale)
    send_groups(out, back, sizes)


def table_cotangents(back, geo, ah, al, gh, gl, vh, vl, cot, filt, height, own_rows, scale):
    channels = filt.shape[1]
    back[...] = jnp.zeros_like(back)

    def chunk(step, _):
        factor = order_factor(step, own_rows)
        scaled_rows(gh, gl, filt, cot[0:own_rows, :], step, slice(None), scale)
        scaled_rows(vh, vl, filt, cot[own_rows:, :], step, slice(None), scale)
        for start in range(0, height, row_block):
            rows = pl.ds(start, row_block)
            s, c = geo[SN, rows, :], geo[CS, rows, :]
            p0 = geo[P0, rows, :]
            put_split(ah, al, start, p0 * s)
            put_split(
                ah,
                al,
                height + start,
                (geo[P1, rows, :] * s + factor * (p0 * c)) * geo[DD, rows, :],
            )
            rotate(geo, rows, s, c)
        top = 2 * height
        both = mxu(ah[:top, :], gh[...]) + mxu(al[:top, :], gh[...]) + mxu(ah[:top, :], gl[...])
        back[:, :channels] += both[:height]
        back[:, channels:] += (
            both[height:]
            + mxu(ah[:height, :], vh[...])
            + mxu(al[:height, :], vh[...])
            + mxu(ah[:height, :], vl[...])
        )
        return 0

    lax.fori_loop(0, filt.shape[0] * own_rows // wide, chunk, 0)


def folded(value, members):
    total = value[:, :lanes] + value[:, lanes:]
    if members < lanes:
        total = total + pltpu.roll(total, members, 1)
    return total


def second_pairs(geo, ah, al, gh, gl, vh, vl, value, dots, filt, members, scale, pair):
    height = geo.shape[1]
    pair[...] = jnp.zeros_like(pair)

    def chunk(step, _):
        factor = order_factor(step, members)
        scaled_rows(gh, gl, filt, value(), step, slice(None), scale)
        scaled_rows(vh, vl, filt, dots(), step, slice(None), scale)
        top = 2 * height
        both = (
            mxu(ah[:top, :], gh[...], nt_dims)
            + mxu(al[:top, :], gh[...], nt_dims)
            + mxu(ah[:top, :], gl[...], nt_dims)
        )
        plain = both[:height]
        dot = (
            both[height:]
            + mxu(ah[:height, :], vh[...], nt_dims)
            + mxu(al[:height, :], vh[...], nt_dims)
            + mxu(ah[:height, :], vl[...], nt_dims)
        )
        for start in range(0, height, row_block):
            rows = pl.ds(start, row_block)
            s, c = geo[SN, rows, :], geo[CS, rows, :]
            p0, p1 = geo[P0, rows, :], geo[P1, rows, :]
            b1 = p1 * s + factor * (p0 * c)
            b2 = geo[P2, rows, :] * s + factor * (2.0 * p1 * c - factor * (p0 * s))
            g = plain[start : start + row_block]
            pair[0, rows, :] += b1 * g
            pair[1, rows, :] += (b2 * geo[DD, rows, :]) * g + b1 * dot[start : start + row_block]
            rotate(geo, rows, s, c)
        return 0

    lax.fori_loop(0, filt.shape[0] * members // wide, chunk, 0)


def second_back_kernel(
    scale,
    pos,
    tan,
    nbr,
    filt,
    coords_ghost,
    phi_two,
    table,
    cot,
    back,
    pair_own,
    pair_ghost,
    box,
    wbox,
    geo,
    ah,
    al,
    gh,
    gl,
    vh,
    vl,
    pair,
):
    own_rows = pos.shape[1]
    channels = filt.shape[1]
    stack_coords(box, pos, tan)
    height = geometry_by_slot(geo, box, wbox, None, nbr, own_rows, False)
    table_cotangents(back, geo, ah, al, gh, gl, vh, vl, cot, filt, height, own_rows, scale)
    put_split(ah, al, 0, cot[...])
    for source, result, ghost in ((phi_two, pair_own, False), (table, pair_ghost, True)):
        members = geometry_by_atom(geo, box, wbox, coords_ghost, nbr, own_rows, ghost)
        second_pairs(
            geo,
            ah,
            al,
            gh,
            gl,
            vh,
            vl,
            lambda: source[:, :channels],
            lambda: source[:, channels:],
            filt,
            members,
            scale,
            pair,
        )
        result[0] = folded(pair[0], members)
        result[1] = folded(pair[1], members)


def first_pairs(geo, ch, cl, gh, gl, vh, vl, phi_ref, filt, members, scale, pair, cots):
    height = geo.shape[1]
    channels = phi_ref.shape[1] // 2
    pair[...] = jnp.zeros_like(pair)

    def chunk(step, _):
        factor = order_factor(step, members)
        scaled_rows(gh, gl, filt, phi_ref[:, :channels], step, slice(0, channels), scale)
        scaled_rows(vh, vl, filt, phi_ref[:, channels:], step, slice(channels, 2 * channels), scale)
        top = 2 * height
        cots[:top, :] = (
            mxu(ch[:top, :], gh[...], nt_dims)
            + mxu(cl[:top, :], gh[...], nt_dims)
            + mxu(ch[:top, :], gl[...], nt_dims)
        )
        cots[top:, :] = (
            mxu(ch[top:, :], vh[...], nt_dims)
            + mxu(cl[top:, :], vh[...], nt_dims)
            + mxu(ch[top:, :], vl[...], nt_dims)
        )
        for start in range(0, height, row_block):
            rows = pl.ds(start, row_block)
            s, c = geo[SN, rows, :], geo[CS, rows, :]
            p0, p1, dd = geo[P0, rows, :], geo[P1, rows, :], geo[DD, rows, :]
            b = p0 * s
            b1 = p1 * s + factor * (p0 * c)
            b2d = (geo[P2, rows, :] * s + factor * (2.0 * p1 * c - factor * b)) * dd
            b1d = b1 * dd
            along = cots[start : start + row_block, :]
            along_dot = cots[height + start : height + start + row_block, :]
            for i in range(3):
                at = (2 + i) * height + start
                g = cots[at : at + row_block, :]
                at = (5 + i) * height + start
                gd = cots[at : at + row_block, :]
                unit = geo[U + i, rows, :]
                along = along + unit * g
                along_dot = along_dot + unit * gd + geo[UD + i, rows, :] * g
                pair[2 + i, rows, :] += b * g
                pair[5 + i, rows, :] += b * gd + b1d * g
            pair[0, rows, :] += b1 * along
            pair[1, rows, :] += b2d * along + b1 * along_dot
            rotate(geo, rows, s, c)
        return 0

    lax.fori_loop(0, filt.shape[0] * members // wide, chunk, 0)


def offset_gradients(geo, pair, second, members, by_slot, by_atom):
    near = [folded(pair[i], members) for i in range(8)]
    height = geo.shape[1]
    units = [geo[U + i, :, :lanes] for i in range(3)]
    moves = [geo[UD + i, :, :lanes] for i in range(3)]
    inverse = geo[RI, :, :lanes]
    speed = geo[DD, :, :lanes]
    along = near[0] + second[0]
    along_dot = near[1] + second[1]
    turn, turn_dot = near[2:5], near[5:8]
    inner = units[0] * turn[0] + units[1] * turn[1] + units[2] * turn[2]
    inner_dot = sum(units[i] * turn_dot[i] + moves[i] * turn[i] for i in range(3))
    rate = speed * inverse
    lane = lax.broadcasted_iota(jnp.int32, (1, lanes), 1)
    sums = jnp.zeros((height, lanes), f32)
    for i in range(3):
        part = (turn[i] - units[i] * inner) * inverse
        grad = along * units[i] + part
        grad_dot = (
            along_dot * units[i]
            + along * moves[i]
            + (turn_dot[i] - moves[i] * inner - units[i] * inner_dot) * inverse
            - rate * part
        )
        for row, value in ((i, grad), (3 + i, grad_dot)):
            by_slot[row : row + 1, :] = jnp.sum(value, 0, keepdims=True)
            if members < lanes:
                value = jnp.where(lane < members, value, 0.0)
            sums = jnp.where(lane == row, -jnp.sum(value, 1, keepdims=True), sums)
    by_atom[...] = sums


def first_back_ghost_kernel(
    sizes,
    scale,
    pos,
    tan,
    nbr,
    send,
    filt,
    coords_ghost,
    phi_ghost,
    cot,
    inner,
    maps,
    back,
    pair_ghost,
    w_two_in,
    w_two_out,
    w_left,
    w_right,
    arrived,
    out,
    bars,
    by_atom,
    box,
    wbox,
    geo,
    ch,
    cl,
    gh,
    gl,
    vh,
    vl,
    pair,
    cots,
    total,
    by_slot,
):
    own_rows = pos.shape[1]
    channels = filt.shape[1] // 2
    stack_coords(box, pos, tan)
    total[...] = back[...]
    add_returned(total, arrived, send, sizes)
    outer = dot3(
        jnp.concatenate([total[:, :channels], total[:, channels:]], 0), w_two_out[...], nt_dims
    )
    _, slope, bend = silu_parts(inner[:own_rows, :])
    pulled = jnp.concatenate(
        [
            outer[:own_rows] * slope,
            outer[own_rows:] * slope + outer[:own_rows] * bend * inner[own_rows:, :],
        ],
        0,
    )
    bars[0 : 2 * own_rows, :] = cot[...] + dot3(pulled, w_two_in[...], nt_dims)
    half = 3 * own_rows
    bar, bar_dot = bars[0:own_rows, :], bars[own_rows : 2 * own_rows, :]
    for i in range(3):
        a, b = i * own_rows, (i + 1) * own_rows
        left, left_dot = maps[a:b, :], maps[half + a : half + b, :]
        right = maps[2 * half + a : 2 * half + b, :]
        right_dot = maps[3 * half + a : 3 * half + b, :]
        for_left = jnp.concatenate([bar * right, bar_dot * right + bar * right_dot], 0)
        for_right = jnp.concatenate([bar * left, bar_dot * left + bar * left_dot], 0)
        both = dot3(for_left, w_left[...], nt_dims) + dot3(for_right, w_right[...], nt_dims)
        at = (2 + i) * own_rows
        bars[at : at + own_rows, :] = both[:own_rows]
        at = (5 + i) * own_rows
        bars[at : at + own_rows, :] = both[own_rows:]
    put_split(ch, cl, 0, bars[...])
    members = geometry_by_atom(geo, box, wbox, coords_ghost, nbr, own_rows, True)
    first_pairs(geo, ch, cl, gh, gl, vh, vl, phi_ghost, filt, members, scale, pair, cots)
    by_slot[...] = jnp.zeros_like(by_slot)
    offset_gradients(geo, pair, pair_ghost, members, by_slot, by_atom)
    for target in offsets:
        device, inside = neighbour_id(target, sizes)

        @pl.when(inside)
        def _():
            out[device] = by_slot[...]


def first_back_own_kernel(
    scale,
    pos,
    tan,
    nbr,
    filt,
    phi_own,
    bars,
    pair_own,
    ghost_sums,
    result,
    box,
    wbox,
    geo,
    ch,
    cl,
    gh,
    gl,
    vh,
    vl,
    pair,
    cots,
    by_atom,
):
    own_rows = pos.shape[1]
    stack_coords(box, pos, tan)
    put_split(ch, cl, 0, bars[...])
    members = geometry_by_atom(geo, box, wbox, None, nbr, own_rows, False)
    first_pairs(geo, ch, cl, gh, gl, vh, vl, phi_own, filt, members, scale, pair, cots)
    result[...] = jnp.zeros_like(result)
    offset_gradients(geo, pair, pair_own, members, result, by_atom)
    result[...] += (by_atom[...] + ghost_sums[...]).T[0:8, :]


def finish_kernel(sizes, send, partial, arrived, forces, product, rows):
    count = send.shape[1] // 8
    own_rows = partial.shape[1]
    rows[...] = jnp.zeros_like(rows)
    lane = lax.broadcasted_iota(jnp.int32, (1, lanes), 1)
    for number, target in enumerate(offsets):
        device, inside = neighbour_id(target, sizes)

        @pl.when(inside)
        def _():
            shift = ((2 * number - 7) * count) % lanes
            moved = arrived[device]
            if shift:
                moved = pltpu.roll(moved, shift, 1)
            mine = (lane >= number * count) & (lane < (number + 1) * count)
            rows[...] += jnp.where(mine, moved, 0.0)

    atom = lax.broadcasted_iota(jnp.int32, (own_rows, 8 * count), 0)
    place = jnp.where(atom == send[...], 1.0, 0.0).astype(bf16)
    value = rows[:, : 8 * count]
    high, low = split(value)
    rest = (value - high.astype(f32) - low.astype(f32)).astype(bf16)
    total = partial[...] + mxu(high, place, nt_dims) + mxu(low, place, nt_dims)
    total = total + mxu(rest, place, nt_dims)
    forces[...] = -total[0:3, :]
    product[...] = -total[3:6, :]


def call(kernel, outs, scratch, name, args, smem=()):
    specs = [
        pl.BlockSpec(memory_space=pltpu.SMEM if i in smem else pltpu.VMEM)
        for i in range(len(args))
    ]
    single = len(outs) == 1
    shapes = [jax.ShapeDtypeStruct(shape, f32) for shape in outs]
    out_specs = [pl.BlockSpec(memory_space=pltpu.VMEM) for _ in outs]
    return pl.pallas_call(
        kernel,
        out_shape=shapes[0] if single else shapes,
        in_specs=specs,
        out_specs=out_specs[0] if single else out_specs,
        scratch_shapes=[pltpu.VMEM(shape, kind) for shape, kind in scratch],
        compiler_params=pltpu.CompilerParams(vmem_limit_bytes=40 * 1024 * 1024),
        name=name,
    )(*args)


def exchanged(buffer):
    return lax.all_to_all(buffer, ("bx", "by"), 0, 0)


def per_device(
    positions,
    tangent,
    embedding,
    counts,
    neighbours,
    send_rows,
    w_one_in,
    w_one_out,
    filter_one,
    w_left,
    w_right,
    w_two_in,
    w_two_out,
    filter_two,
    w_hidden,
    w_energy,
):
    sizes = (lax.axis_size("bx"), lax.axis_size("by"))
    devices = sizes[0] * sizes[1]
    n = positions.shape[1]
    channels = embedding.shape[1]
    ghosts = send_rows.shape[1]
    count = ghosts // 8
    scale = 1.0 / math.sqrt(neighbours.shape[0])
    part = functools.partial
    base = [((n, n), f32), ((n, wide), f32), ((geo_slots, n, wide), f32)]

    def halves(rows):
        return [((rows, wide), bf16)] * 2

    factors = halves(wide) + halves(wide)

    buffer = call(
        part(pack_kernel, sizes),
        [(devices, count, channels + lanes)],
        [((n, n), f32), ((n, channels + lanes), f32)],
        "pack",
        (positions, tangent, embedding, send_rows),
        (3,),
    )
    arrived = exchanged(buffer)
    partial, phi_own = call(
        part(first_own_kernel, scale),
        [(8 * n, channels), (n, 2 * channels)],
        base + halves(8 * n) + factors,
        "first_own",
        (positions, tangent, embedding, neighbours, w_one_in, w_one_out, filter_one),
    )
    buffer, state, inner, maps, phi_two, phi_ghost, coords_ghost = call(
        part(first_ghost_kernel, sizes, scale),
        [
            (devices, count, 2 * channels),
            (2 * n, channels),
            (2 * n, channels),
            (12 * n, channels),
            (n, 2 * channels),
            (ghosts, 2 * channels),
            (ghosts, lanes),
        ],
        base
        + halves(8 * n)
        + factors
        + [((8 * n, channels), f32), ((ghosts, channels + lanes), f32)],
        "first_ghost",
        (
            positions,
            tangent,
            embedding,
            neighbours,
            send_rows,
            w_one_in,
            w_one_out,
            filter_one,
            w_left,
            w_right,
            w_two_in,
            w_two_out,
            partial,
            arrived,
        ),
        (4,),
    )
    arrived = exchanged(buffer)
    partial = call(
        part(second_own_kernel, scale),
        [(2 * n, channels)],
        base + halves(2 * n) + factors,
        "second_own",
        (positions, tangent, neighbours, filter_two, phi_two),
    )
    buffer, table, cot = call(
        part(second_ghost_kernel, sizes, scale),
        [(devices, count, 2 * channels), (ghosts, 2 * channels), (2 * n, channels)],
        base
        + halves(2 * n)
        + factors
        + [((2 * n, channels), f32), ((ghosts, 2 * channels), f32)],
        "second_ghost",
        (
            positions,
            tangent,
            neighbours,
            counts,
            filter_two,
            coords_ghost,
            state,
            partial,
            w_hidden,
            w_energy.reshape(1, channels),
            arrived,
        ),
        (3,),
    )
    arrived = exchanged(buffer)
    back, pair_own, pair_ghost = call(
        part(second_back_kernel, scale),
        [(n, 2 * channels), (2, n, lanes), (2, n, lanes)],
        base + halves(2 * n) + factors + [((2, n, wide), f32)],
        "second_back",
        (positions, tangent, neighbours, filter_two, coords_ghost, phi_two, table, cot),
    )
    pairs = [((8, n, wide), f32), ((8 * n, wide), f32)]
    buffer, bars, ghost_sums = call(
        part(first_back_ghost_kernel, sizes, scale),
        [(devices, 8, lanes), (8 * n, channels), (n, lanes)],
        base
        + halves(8 * n)
        + factors
        + pairs
        + [((n, 2 * channels), f32), ((8, lanes), f32)],
        "first_back_ghost",
        (
            positions,
            tangent,
            neighbours,
            send_rows,
            filter_one,
            coords_ghost,
            phi_ghost,
            cot,
            inner,
            maps,
            back,
            pair_ghost,
            w_two_in,
            w_two_out,
            w_left,
            w_right,
            arrived,
        ),
        (3,),
    )
    arrived = exchanged(buffer)
    partial = call(
        part(first_back_own_kernel, scale),
        [(8, lanes)],
        base + halves(8 * n) + factors + pairs + [((n, lanes), f32)],
        "first_back_own",
        (
            positions,
            tangent,
            neighbours,
            filter_one,
            phi_own,
            bars,
            pair_own,
            ghost_sums,
        ),
    )
    return call(
        part(finish_kernel, sizes),
        [(3, n), (3, n)],
        [((8, lanes), f32)],
        "finish",
        (send_rows, partial, arrived),
    )


def solution(mesh):
    placed = (
        P(None, ("bx", "by")),
        P(None, ("bx", "by")),
        P(("bx", "by"), None),
        P(("bx", "by")),
        P(None, ("bx", "by")),
        P(("bx", "by"), None),
        P(),
        P(),
        P(),
        P(),
        P(),
        P(),
        P(),
        P(),
        P(),
        P(),
    )

    def run(*arrays):
        return tuple(per_device(*arrays))

    return jax.shard_map(
        run,
        mesh=mesh,
        in_specs=placed,
        out_specs=(P(None, ("bx", "by")), P(None, ("bx", "by"))),
        check_vma=False,
    )
```

time: 604 us -> 122 us (0.20); the launches traced: 595 us -> 119 us
  other arithmetic: 196 us -> 0 us
  matrix products: 147 us -> 0 us
  local copies, waits for them, and re-layouts: 134 us -> 33.2 us
  starting transfers between devices: 104 us -> 20.5 us
  Pallas kernels: 0 us -> 53.1 us
    dot_general x39 -> x0, matrix products: 147 us -> none  [the longest x8 80.4 us: edge_weights(): mixed = jnp.einsum('qkr,qc->krc', radial, filter_table, precision=highest)]
    scatter-add x10 -> x0, other arithmetic: 142 us -> none  [the longest x4 90.3 us: geometry(): others = jnp.take(pos_table, own_lists, axis=1)]
    ppermute x32 -> x0, starting transfers between devices: 104 us -> none  [passed_along(): return lax.ppermute(block, axis, route)]
    gather x39 -> x0, local copies, waits for them, and re-layouts: 102 us -> none  [the longest x2 32.5 us: second_layer(): jnp.take(phi_table, own_lists, axis=0)]
    pallas_call x0 -> x9, Pallas kernels: none -> 53.1 us  [call(): pl.pallas_call(kernel, out_shape=shapes[0] if single else shapes, in_spec...]
    unnamed x230 -> x106, local copies, waits for them, and re-layouts: 4.47 us -> 33.2 us
    reduce_sum x7 -> x0, other arithmetic: 26.4 us -> none  [the longest x2 21.4 us: edge_weights(): return mixed * envelope[:, :, None]]
    all_to_all x0 -> x4, starting transfers between devices: none -> 20.5 us  [exchanged(): return lax.all_to_all(buffer, ('bx', 'by'), 0, 0)]
  transfers between devices with their start and end apart: 32 -> 4, of which waited for: 4 -> 2; matrix products, arithmetic and copies ran while one was open for 31% -> 0% of each run, Pallas kernels for 0% -> 26%
where the time goes in v1:
time: 122 us; the launch traced here: 119 us
  Pallas kernels  53.1 us (44%)
  local copies, waits for them, and re-layouts  33.2 us (27%)
  starting transfers between devices  20.5 us (17%)
  waiting for transfers between devices  11 us (9%)
  between operations  1.59 us (1%)
    pallas_call x9, Pallas kernels, call(): pl.pallas_call(kernel, out_shape=shapes[0] if single else shapes, in_spec...  53.1 us
    unnamed x106, local copies, waits for them, and re-layouts  33.2 us
    all_to_all x4, starting transfers between devices, exchanged(): return lax.all_to_all(buffer, ('bx', 'by'), 0, 0)  20.5 us
    all_to_all x4, waiting for transfers between devices, exchanged(): return lax.all_to_all(buffer, ('bx', 'by'), 0, 0)  11 us
  transfers between devices with their start and end apart: 4, of which 2 were waited for; matrix products, arithmetic and copies ran while one was open for 0% of the time, Pallas kernels for 26%

profile of v1, /device:TPU:4, one launch (start us, length us, event | category | flops | bytes accessed | tf_op | source)
XLA Modules:
  0.0 119.4 jit_solution(4275414272883940866)
XLA Ops:
  0.7 1.0 copy-done.1
  3.7 1.5 %pack.1 = f32[32,8,384]{2,1,0:T(8,128)} custom-call(f32[3,128]{1,0:T(4,128)S(1)} %copy-done.42, f32[3,128]{1,0:T(4,128)S(1)} %copy-done.45, f32[128,256]{1,0:T(8,128)S(1)} %copy-done.1, s32[1,64]{1,0:T(1,128)S(1)} %copy-done.50), custom_call_target="tpu_custom_call" | custom-call | tf_op jit(solution)/shard_map/pack/pallas_call | solution.py:853
  5.2 6.1 %all-to-all-start = ((f32[32,8,384]{2,1,0:T(8,128)}), f32[32,8,384]{2,1,0:T(8,128)S(1)}, u32[]{:S(2)}, u32[]{:S(2)}) async-start(f32[32,8,384]{2,1,0:T(8,128)} %pack.1), calls=%async_computation | async-start | bytes 786432 | tf_op jit(solution)/shard_map/all_to_all | solution.py:865
  12.2 0.9 copy-done.6
  16.0 7.4 %first_own.1 = (f32[1024,256]{1,0:T(8,128)S(1)}, f32[128,512]{1,0:T(8,128)S(1)}) custom-call(f32[3,128]{1,0:T(4,128)S(1)} %copy-done.43, f32[3,128]{1,0:T(4,128)S(1)} %copy-done.46, f32[128,256]{1,0:T(8,128)S(1)} %copy-done.2, s32[32,128]{1,0:T(8,128)S(1)} %copy-done.17, f32[256,256]{1,0:T(8,128)S(1)} %copy-done.6, f32[256,512]{1,0:T(8,128)S(1)} %copy-done, ...), custom_call_target="tpu_custom_call" | custom-call | tf_op jit(solution)/shard_map/first_own/pallas_call | solution.py:853
  23.5 1.0 copy-done.4
  25.3 1.2 %copy-done.5 = f32[1024,256]{1,0:T(8,128)S(1)} copy-done((f32[1024,256]{1,0:T(8,128)S(1)}, f32[1024,256]{1,0:T(8,128)}, u32[]{:S(2)}) %copy-start.5) | copy-done | bytes 1048600
  27.4 0.9 copy-done.11
  28.4 0.9 copy-done.13
  29.4 6.0 %first_ghost.1 = (f32[32,8,512]{2,1,0:T(8,128)S(1)}, f32[256,256]{1,0:T(8,128)S(1)}, f32[256,256]{1,0:T(8,128)S(1)}, f32[1536,256]{1,0:T(8,128)S(1)}, f32[128,51...) custom-call(f32[3,128]{1,0:T(4,128)S(1)} %copy-done.44, f32[3,128]{1,0:T(4,128)S(1)} %copy-done.47, ...), custom_call_target="tpu_custom_call" | custom-call | tf_op jit(solution)/shard_map/first_ghost/pallas_call | solution.py:853
  38.2 5.8 %all-to-all-start.1 = ((f32[32,8,512]{2,1,0:T(8,128)}), f32[32,8,512]{2,1,0:T(8,128)S(1)}, u32[]{:S(2)}, u32[]{:S(2)}) async-start(f32[32,8,512]{2,1,0:T(8,128)} %copy-done.22), calls=%async_computation.1 | async-start | bytes 1048576 | tf_op jit(solution)/shard_map/all_to_all | solution.py:865
  44.7 4.2 %second_own.1.partial = f32[256,256]{1,0:T(8,128)S(1)} custom-call(f32[3,128]{1,0:T(4,128)S(1)} %copy-done.44, f32[3,128]{1,0:T(4,128)S(1)} %copy-done.47, s32[32,128]{1,0:T(8,128)S(1)} %copy-done.18, f32[20,256]{1,0:T(8,128)S(1)} %copy-done.32, f32[128,512]{1,0:T(8,128)S(1)} %get-tuple-element.25.phi_two), custom_call_target="tpu_custom_call" | custom-call | tf_op jit(solution)/shard_map/second_own/pallas_call | solution.py:853
  48.9 10.2 %all-to-all-done.1.arrived = f32[32,8,512]{2,1,0:T(8,128)S(1)} async-done(((f32[32,8,512]{2,1,0:T(8,128)}), f32[32,8,512]{2,1,0:T(8,128)S(1)}, u32[]{:S(2)}, u32[]{:S(2)}) %all-to-all-start.1) | async-done | bytes 524320 | tf_op jit(solution)/shard_map/all_to_all | solution.py:865
  59.1 0.9 copy-done.27
  60.0 5.9 %second_ghost.1 = (f32[32,8,512]{2,1,0:T(8,128)S(1)}, f32[64,512]{1,0:T(8,128)S(1)}, f32[256,256]{1,0:T(8,128)S(1)}) custom-call(f32[3,128]{1,0:T(4,128)S(1)} %copy-done.44, f32[3,128]{1,0:T(4,128)S(1)} %copy-done.47, s32[32,128]{1,0:T(8,128)S(1)} %copy-done.18, s32[1]{0:T(128)S(6)} %copy.18.counts, f32[20,256]{1,0:T(8,128)S(1)} %copy-done.32, ...), custom_call_target="tpu_custom_call" | custom-call | tf_op jit(solution)/shard_map/second_ghost/pallas_call | solution.py:853
  67.4 3.6 %all-to-all-start.2 = ((f32[32,8,512]{2,1,0:T(8,128)}), f32[32,8,512]{2,1,0:T(8,128)S(1)}, u32[]{:S(2)}, u32[]{:S(2)}) async-start(f32[32,8,512]{2,1,0:T(8,128)} %copy-done.21), calls=%async_computation.2 | async-start | bytes 1048576 | tf_op jit(solution)/shard_map/all_to_all | solution.py:865
  71.9 11.2 %second_back.1 = (f32[128,512]{1,0:T(8,128)S(1)}, f32[2,128,128]{2,1,0:T(8,128)S(1)}, f32[2,128,128]{2,1,0:T(8,128)S(1)}) custom-call(f32[3,128]{1,0:T(4,128)S(1)} %copy-done.44, f32[3,128]{1,0:T(4,128)S(1)} %copy-done.47, s32[32,128]{1,0:T(8,128)S(1)} %copy-done.18, f32[20,256]{1,0:T(8,128)S(1)} %copy-done.32, ...), custom_call_target="tpu_custom_call" | custom-call | tf_op jit(solution)/shard_map/second_back/pallas_call | solution.py:853
  86.0 0.9 copy-done.10
  87.0 0.9 copy-done.12
  87.9 0.9 copy-done.14
  93.5 7.0 %first_back_ghost.1 = (f32[32,8,128]{2,1,0:T(8,128)S(1)}, f32[1024,256]{1,0:T(8,128)S(1)}, f32[128,128]{1,0:T(8,128)S(1)}) custom-call(f32[3,128]{1,0:T(4,128)S(1)} %copy-done.44, f32[3,128]{1,0:T(4,128)S(1)} %copy-done.47, s32[32,128]{1,0:T(8,128)S(1)} %copy-done.18, s32[1,64]{1,0:T(1,128)S(1)} %copy-done.51, f32[20,512]{1,0:T(8,128)S(1)} %copy-done.20, ...), custom_call_target="tpu_custom_call" | custom-call | tf_op jit(solution)/shard_map/first_back_ghost/pallas_call | solution.py:853
  101.8 5.0 %all-to-all-start.3 = ((f32[32,8,128]{2,1,0:T(8,128)}), f32[32,8,128]{2,1,0:T(8,128)S(1)}, u32[]{:S(2)}, u32[]{:S(2)}) async-start(f32[32,8,128]{2,1,0:T(8,128)} %copy-done.35), calls=%async_computation.3 | async-start | bytes 262144 | tf_op jit(solution)/shard_map/all_to_all | solution.py:865
  109.5 8.8 %first_back_own.1.partial = f32[8,128]{1,0:T(8,128)S(1)} custom-call(f32[3,128]{1,0:T(4,128)S(1)} %copy-done.44, f32[3,128]{1,0:T(4,128)S(1)} %copy-done.47, s32[32,128]{1,0:T(8,128)S(1)} %copy-done.18, f32[20,512]{1,0:T(8,128)S(1)} %copy-done.20, f32[128,512]{1,0:T(8,128)S(1)} %copy-done.25, f32[1024,256]{1,0:T(8,128)S(1)} %get-tuple-element.34.bars, ...), custom_call_target="tpu_custom_call" | custom-call | tf_op jit(solution)/shard_map/first_back_own/pallas_call | solution.py:853
  118.2 1.2 finish.1
  (99 shorter events, 24.2 us)
Async XLA Ops:
  0.6 10.7 %copy-start = (f32[256,512]{1,0:T(8,128)S(1)}, f32[256,512]{1,0:T(8,128)}, u32[]{:S(2)}) copy-start(f32[256,512]{1,0:T(8,128)} %w_out.3) | copy-start | bytes 1572868
  0.6 1.0 copy-start.1
  3.6 21.6 %copy-start.3 = (f32[128,256]{1,0:T(8,128)S(1)}, f32[128,256]{1,0:T(8,128)}, u32[]{:S(2)}) copy-start(f32[128,256]{1,0:T(8,128)} %emb.5) | copy-start | bytes 393220
  3.6 21.6 %copy-start.7 = (f32[256,256]{1,0:T(8,128)S(1)}, f32[256,256]{1,0:T(8,128)}, u32[]{:S(2)}) copy-start(f32[256,256]{1,0:T(8,128)} %w_in.3) | copy-start | bytes 786436
  3.6 21.6 %copy-start.8 = (f32[256,256]{1,0:T(8,128)S(1)}, f32[256,256]{1,0:T(8,128)}, u32[]{:S(2)}) copy-start(f32[256,256]{1,0:T(8,128)} %w_left.3) | copy-start | bytes 786436
  3.6 21.6 %copy-start.18 = (s32[32,128]{1,0:T(8,128)S(1)}, s32[32,128]{1,0:T(8,128)}, u32[]{:S(2)}) copy-start(s32[32,128]{1,0:T(8,128)} %nbr.13) | copy-start | bytes 49156
  3.6 21.6 %copy-start.20 = (f32[20,512]{1,0:T(8,128)S(1)}, f32[20,512]{1,0:T(8,128)}, u32[]{:S(2)}) copy-start(f32[20,512]{1,0:T(8,128)} %filt.13) | copy-start | bytes 122884
  3.6 21.6 %copy-start.44 = (f32[3,128]{1,0:T(4,128)S(1)}, f32[3,128]{1,0:T(4,128)}, u32[]{:S(2)}) copy-start(f32[3,128]{1,0:T(4,128)} %pos.15) | copy-start | bytes 4612
  3.7 21.6 %copy-start.47 = (f32[3,128]{1,0:T(4,128)S(1)}, f32[3,128]{1,0:T(4,128)}, u32[]{:S(2)}) copy-start(f32[3,128]{1,0:T(4,128)} %tan.15) | copy-start | bytes 4612
  3.7 21.6 %copy-start.51 = (s32[1,64]{1,0:T(1,128)S(1)}, s32[1,64]{1,0:T(1,128)}, u32[]{:S(2)}) copy-start(s32[1,64]{1,0:T(1,128)} %send.7) | copy-start | bytes 772
  5.2 20.0 %all-to-all-start = ((f32[32,8,384]{2,1,0:T(8,128)}), f32[32,8,384]{2,1,0:T(8,128)S(1)}, u32[]{:S(2)}, u32[]{:S(2)}) async-start(f32[32,8,384]{2,1,0:T(8,128)} %pack.1), calls=%async_computation | async-start | bytes 786432 | tf_op jit(solution)/shard_map/all_to_all | solution.py:865
  12.2 0.9 copy-start.6
  23.5 1.0 copy-start.4
  25.3 1.2 %copy-start.5 = (f32[1024,256]{1,0:T(8,128)S(1)}, f32[1024,256]{1,0:T(8,128)}, u32[]{:S(2)}) copy-start(f32[1024,256]{1,0:T(8,128)} %copy-done.4) | copy-start | bytes 3145732
  29.3 15.3 %copy-start.32 = (f32[20,256]{1,0:T(8,128)S(1)}, f32[20,256]{1,0:T(8,128)}, u32[]{:S(2)}) copy-start(f32[20,256]{1,0:T(8,128)} %filt.11) | copy-start | bytes 61444
  38.2 20.9 %copy-start.23 = (f32[256,256]{1,0:T(8,128)S(1)}, f32[256,256]{1,0:T(8,128)}, u32[]{:S(2)}) copy-start(f32[256,256]{1,0:T(8,128)} %w_hidden.1) | copy-start | bytes 786436
  38.2 20.9 %copy-start.52 = (f32[256]{0:T(256)S(1)}, f32[256]{0:T(256)}, u32[]{:S(2)}) copy-start(f32[256]{0:T(256)} %param.31) | copy-start | bytes 3076
  38.2 20.9 %all-to-all-start.1 = ((f32[32,8,512]{2,1,0:T(8,128)}), f32[32,8,512]{2,1,0:T(8,128)S(1)}, u32[]{:S(2)}, u32[]{:S(2)}) async-start(f32[32,8,512]{2,1,0:T(8,128)} %copy-done.22), calls=%async_computation.1 | async-start | bytes 1048576 | tf_op jit(solution)/shard_map/all_to_all | solution.py:865
  59.1 1.0 copy-start.27
  67.4 18.6 %copy-start.15 = (f32[256,256]{1,0:T(8,128)}, f32[256,256]{1,0:T(8,128)S(1)}, u32[]{:S(2)}) copy-start(f32[256,256]{1,0:T(8,128)S(1)} %get-tuple-element.27.cot) | copy-start | bytes 786436
  67.4 18.6 %all-to-all-start.2 = ((f32[32,8,512]{2,1,0:T(8,128)}), f32[32,8,512]{2,1,0:T(8,128)S(1)}, u32[]{:S(2)}, u32[]{:S(2)}) async-start(f32[32,8,512]{2,1,0:T(8,128)} %copy-done.21), calls=%async_computation.2 | async-start | bytes 1048576 | tf_op jit(solution)/shard_map/all_to_all | solution.py:865
  86.0 1.0 copy-start.10
  101.8 16.4 %all-to-all-start.3 = ((f32[32,8,128]{2,1,0:T(8,128)}), f32[32,8,128]{2,1,0:T(8,128)S(1)}, u32[]{:S(2)}, u32[]{:S(2)}) async-start(f32[32,8,128]{2,1,0:T(8,128)} %copy-done.35), calls=%async_computation.3 | async-start | bytes 262144 | tf_op jit(solution)/shard_map/all_to_all | solution.py:865
  106.8 1.0 copy-start.25
  (33 other events, 26.2 us)
